TPU v7x, 128 devices: a whole 4x4x4 slice. The times are simulated.
128 devices in a mesh: blk: 16 (over y_hi, z, core), freq: 8 (over y_lo, x).
Axes of the slice: x: 4, y: 4 (y_hi: 2, y_lo: 2; y = y_hi * 2 + y_lo), z: 4, core: 2. Of those that a mesh axis runs over, the one named last changes fastest.
Arguments:
- spectra: bfloat16 [5120, 34816], P('blk', 'freq'), may hold values from -16 to 16, as said below
- labels: int32 [5120], replicated, may hold values from 0 to 7
- wedges: int32 [8, 17408], P(None, 'freq'), may hold values 0 or 1
- shells: int32 [17408], P('freq'), may hold values from 0 to 27, never falling along the last dimension, each value on 1 to 1243 neighbouring positions
- shell_weight: float32 [28], replicated, may hold values from 0.2 to 5
Outputs:
- scores: float32 [5120, 5120], P('blk', 'freq')
Inputs may be any that keep to these rules, and one draw needn't show every extreme that they name: `spectra`: finite values. `shells`: never falling along the voxels; each shell has 1 to 1243 voxels.
All inputs are finite; a program needn't handle non-finite values. No bound on the sum of `wedges` on one device may be relied on, other than what follows from the above.
Results may differ from a plain program's by a relative error of at most 0.0003.
Values may be sent and summed in bfloat16 or wider, within the bound.
No kernel may reach another device: no remote copies, remote signals or barrier semaphores. Data moves between devices by JAX's collectives and lax.ppermute only.
A program may use at most 128 MiB of HBM per device.

v0:
```python
import jax
import jax.numpy as jnp
from jax import lax
from jax.sharding import PartitionSpec as P


def passed_along(block, axis, distance):
    devices = range(lax.axis_size(axis))
    route = [((i - distance) % len(devices), i) for i in devices]
    return lax.ppermute(block, axis, route)


def advance(visitor):
    return passed_along(visitor, "blk", -1)


def per_device(spectra, labels, wedges, shells, shell_weight):
    cycle_size = lax.axis_size("blk")
    half_cycle = cycle_size // 2
    own_index = lax.axis_index("blk")
    row_count = spectra.shape[0]
    classes = wedges.shape[0]
    shell_count = shell_weight.shape[0]
    class_range = jnp.arange(classes, dtype=jnp.int32)
    own_labels = lax.dynamic_slice_in_dim(labels, own_index * row_count, row_count)
    own_hot = (own_labels[:, None] == class_range[None, :]).astype(jnp.float32)
    wedge_pairs = jnp.repeat(wedges, 2, axis=1)
    keep_mask = jnp.dot(
        own_hot.astype(jnp.bfloat16),
        wedge_pairs.astype(jnp.bfloat16),
        preferred_element_type=jnp.float32,
    )
    masked = spectra * keep_mask.astype(jnp.bfloat16)
    shell_hot = (shells[:, None] == jnp.arange(shell_count, dtype=jnp.int32)[None, :]).astype(
        jnp.float32
    )
    voxel_weight = jnp.dot(shell_hot, shell_weight, precision=lax.Precision.HIGHEST)
    pair_weight = jnp.repeat(voxel_weight, 2)
    weighted = (masked.astype(jnp.float32) * pair_weight).astype(jnp.bfloat16)
    squares = masked.astype(jnp.float32) ** 2 * pair_weight
    partial_energy = jnp.dot(
        squares, wedge_pairs.astype(jnp.float32).T, precision=lax.Precision.HIGHEST
    )
    energy_rows = lax.psum(partial_energy, "freq")
    energy_all = lax.all_gather(energy_rows, "blk", axis=0, tiled=True)
    lower_half = own_index < half_cycle

    def record(stacks, visitor, offset):
        own_stack, back_stack = stacks
        gram_tile = lax.dot_general(
            weighted, visitor, (((1,), (1,)), ((), ())), preferred_element_type=jnp.float32
        )
        slot_index = (own_index + offset) % cycle_size
        at_half = offset == half_cycle
        keeping = jnp.logical_or(jnp.logical_not(at_half), lower_half)
        kept = jnp.where(keeping, gram_tile, jnp.zeros_like(gram_tile))
        own_stack = lax.dynamic_update_index_in_dim(own_stack, kept, slot_index, 0)
        middle = jnp.logical_and(offset > 0, offset < half_cycle)
        sending = jnp.logical_or(middle, jnp.logical_and(at_half, lower_half))
        returned = jnp.where(sending, gram_tile.T, jnp.zeros_like(gram_tile))
        back_stack = lax.dynamic_update_index_in_dim(back_stack, returned, slot_index, 0)
        return (own_stack, back_stack)

    empty = jnp.zeros((cycle_size, row_count, row_count), jnp.float32)
    stacks = record((empty, empty), masked, 0)

    def one_step(offset, carry):
        inner, visitor = carry
        visitor = advance(visitor)
        return (record(inner, visitor, offset), visitor)

    stacks, visitor = lax.fori_loop(1, half_cycle + 1, one_step, (stacks, masked))
    own_stack, back_stack = stacks
    received = lax.all_to_all(back_stack, "blk", split_axis=0, concat_axis=0, tiled=True)
    combined = own_stack + received
    reduced = lax.psum_scatter(combined, "freq", scatter_dimension=0, tiled=True)
    groups = reduced.shape[0]
    first_block = lax.axis_index("freq") * groups
    column_labels = lax.dynamic_slice_in_dim(
        labels.reshape(cycle_size, row_count), first_block, groups, 0
    )
    column_hot = (column_labels[:, :, None] == class_range[None, None, :]).astype(jnp.float32)
    column_energy = lax.dynamic_slice_in_dim(
        energy_all.reshape(cycle_size, row_count, classes), first_block, groups, 0
    )
    row_side = jnp.einsum("id,gjd->gij", energy_rows, column_hot, precision=lax.Precision.HIGHEST)
    column_side = jnp.einsum("gjd,id->gij", column_energy, own_hot, precision=lax.Precision.HIGHEST)
    normed = reduced / jnp.sqrt(row_side * column_side + 1e-06)
    return jnp.transpose(normed, (1, 0, 2)).reshape(row_count, groups * row_count)


def solution(mesh):
    placed = (P("blk", "freq"), P(), P(None, "freq"), P("freq"), P())
    return jax.shard_map(
        per_device, mesh=mesh, in_specs=placed, out_specs=P("blk", "freq"), check_vma=False
    )
```

profile of v0, /device:TPU:1, one launch (start us, length us, event | category | flops | bytes accessed | tf_op | source)
XLA Modules:
  0.0 613.2 jit_solution(9574984736134157134)
XLA Ops:
  10.3 5.8 broadcast_in_dim.45
  16.1 4.4 fusion.1
  32.4 334.9 %while.19 = (s32[]{:T(128)}, f32[16,320,320]{1,2,0:T(8,128)}, f32[16,320,320]{1,2,0:T(8,128)}, bf16[320,4352]{1,0:T(8,128)(2,1)}, pred[]{:T(512)}, /*index=5*/bf...) while((s32[]{:T(128)}, f32[16,320,320]{1,2,0:T(8,128)}, ...), condition=%wide.region_1.2_spmd, body=%wide.region_0.0_spmd.sunk | while | flops 891494400 | bytes 25723240 | solution.py:72
  33.8 33.0 %collective-permute-done = bf16[320,4352]{1,0:T(8,128)(2,1)S(1)} collective-permute-done((bf16[320,4352]{1,0:T(8,128)(2,1)}, bf16[320,4352]{1,0:T(8,128)(2,1)S(1)}, u32[]{:S(2)}, u32[]{:S(2)}) %collective-permute-start) | collective-permute-done | bytes 2785312 | tf_op jit(solution)/shard_map/while/body/eval_jaxpr/ppermute | solution.py:10
  75.5 4.4 collective-permute-start
  79.9 28.6 %collective-permute-done = bf16[320,4352]{1,0:T(8,128)(2,1)S(1)} collective-permute-done((bf16[320,4352]{1,0:T(8,128)(2,1)}, bf16[320,4352]{1,0:T(8,128)(2,1)S(1)}, u32[]{:S(2)}, u32[]{:S(2)}) %collective-permute-start) | collective-permute-done | bytes 2785312 | tf_op jit(solution)/shard_map/while/body/eval_jaxpr/ppermute | solution.py:10
  117.2 8.1 %collective-permute-start = (bf16[320,4352]{1,0:T(8,128)(2,1)}, bf16[320,4352]{1,0:T(8,128)(2,1)S(1)}, u32[]{:S(2)}, u32[]{:S(2)}) collective-permute-start(bf16[320,4352]{1,0:T(8,128)(2,1)} %get-tuple-element.288), channel_id=1, source_target_pairs={{8,0},{16,8},{24,16},{32,24},{40,32},{48,40},{56,48},{64,56},{72,6... | collective-permute-start | bytes 8355848 | tf_op jit(solution)/shard_map/while/body/eval_jaxpr/ppermute | solution.py:10
  125.3 24.9 %collective-permute-done = bf16[320,4352]{1,0:T(8,128)(2,1)S(1)} collective-permute-done((bf16[320,4352]{1,0:T(8,128)(2,1)}, bf16[320,4352]{1,0:T(8,128)(2,1)S(1)}, u32[]{:S(2)}, u32[]{:S(2)}) %collective-permute-start) | collective-permute-done | bytes 2785312 | tf_op jit(solution)/shard_map/while/body/eval_jaxpr/ppermute | solution.py:10
  158.8 11.7 %collective-permute-start = (bf16[320,4352]{1,0:T(8,128)(2,1)}, bf16[320,4352]{1,0:T(8,128)(2,1)S(1)}, u32[]{:S(2)}, u32[]{:S(2)}) collective-permute-start(bf16[320,4352]{1,0:T(8,128)(2,1)} %get-tuple-element.288), channel_id=1, source_target_pairs={{8,0},{16,8},{24,16},{32,24},{40,32},{48,40},{56,48},{64,56},{72,6... | collective-permute-start | bytes 8355848 | tf_op jit(solution)/shard_map/while/body/eval_jaxpr/ppermute | solution.py:10
  170.5 21.4 %collective-permute-done = bf16[320,4352]{1,0:T(8,128)(2,1)S(1)} collective-permute-done((bf16[320,4352]{1,0:T(8,128)(2,1)}, bf16[320,4352]{1,0:T(8,128)(2,1)S(1)}, u32[]{:S(2)}, u32[]{:S(2)}) %collective-permute-start) | collective-permute-done | bytes 2785312 | tf_op jit(solution)/shard_map/while/body/eval_jaxpr/ppermute | solution.py:10
  200.6 15.3 %collective-permute-start = (bf16[320,4352]{1,0:T(8,128)(2,1)}, bf16[320,4352]{1,0:T(8,128)(2,1)S(1)}, u32[]{:S(2)}, u32[]{:S(2)}) collective-permute-start(bf16[320,4352]{1,0:T(8,128)(2,1)} %get-tuple-element.288), channel_id=1, source_target_pairs={{8,0},{16,8},{24,16},{32,24},{40,32},{48,40},{56,48},{64,56},{72,6... | collective-permute-start | bytes 8355848 | tf_op jit(solution)/shard_map/while/body/eval_jaxpr/ppermute | solution.py:10
  215.9 17.7 %collective-permute-done = bf16[320,4352]{1,0:T(8,128)(2,1)S(1)} collective-permute-done((bf16[320,4352]{1,0:T(8,128)(2,1)}, bf16[320,4352]{1,0:T(8,128)(2,1)S(1)}, u32[]{:S(2)}, u32[]{:S(2)}) %collective-permute-start) | collective-permute-done | bytes 2785312 | tf_op jit(solution)/shard_map/while/body/eval_jaxpr/ppermute | solution.py:10
  242.2 19.0 %collective-permute-start = (bf16[320,4352]{1,0:T(8,128)(2,1)}, bf16[320,4352]{1,0:T(8,128)(2,1)S(1)}, u32[]{:S(2)}, u32[]{:S(2)}) collective-permute-start(bf16[320,4352]{1,0:T(8,128)(2,1)} %get-tuple-element.288), channel_id=1, source_target_pairs={{8,0},{16,8},{24,16},{32,24},{40,32},{48,40},{56,48},{64,56},{72,6... | collective-permute-start | bytes 8355848 | tf_op jit(solution)/shard_map/while/body/eval_jaxpr/ppermute | solution.py:10
  261.2 14.1 %collective-permute-done = bf16[320,4352]{1,0:T(8,128)(2,1)S(1)} collective-permute-done((bf16[320,4352]{1,0:T(8,128)(2,1)}, bf16[320,4352]{1,0:T(8,128)(2,1)S(1)}, u32[]{:S(2)}, u32[]{:S(2)}) %collective-permute-start) | collective-permute-done | bytes 2785312 | tf_op jit(solution)/shard_map/while/body/eval_jaxpr/ppermute | solution.py:10
  283.9 22.6 %collective-permute-start = (bf16[320,4352]{1,0:T(8,128)(2,1)}, bf16[320,4352]{1,0:T(8,128)(2,1)S(1)}, u32[]{:S(2)}, u32[]{:S(2)}) collective-permute-start(bf16[320,4352]{1,0:T(8,128)(2,1)} %get-tuple-element.288), channel_id=1, source_target_pairs={{8,0},{16,8},{24,16},{32,24},{40,32},{48,40},{56,48},{64,56},{72,6... | collective-permute-start | bytes 8355848 | tf_op jit(solution)/shard_map/while/body/eval_jaxpr/ppermute | solution.py:10
  306.5 10.5 %collective-permute-done = bf16[320,4352]{1,0:T(8,128)(2,1)S(1)} collective-permute-done((bf16[320,4352]{1,0:T(8,128)(2,1)}, bf16[320,4352]{1,0:T(8,128)(2,1)S(1)}, u32[]{:S(2)}, u32[]{:S(2)}) %collective-permute-start) | collective-permute-done | bytes 2785312 | tf_op jit(solution)/shard_map/while/body/eval_jaxpr/ppermute | solution.py:10
  325.6 26.2 %collective-permute-start = (bf16[320,4352]{1,0:T(8,128)(2,1)}, bf16[320,4352]{1,0:T(8,128)(2,1)S(1)}, u32[]{:S(2)}, u32[]{:S(2)}) collective-permute-start(bf16[320,4352]{1,0:T(8,128)(2,1)} %get-tuple-element.288), channel_id=1, source_target_pairs={{8,0},{16,8},{24,16},{32,24},{40,32},{48,40},{56,48},{64,56},{72,6... | collective-permute-start | bytes 8355848 | tf_op jit(solution)/shard_map/while/body/eval_jaxpr/ppermute | solution.py:10
  351.8 6.8 %collective-permute-done = bf16[320,4352]{1,0:T(8,128)(2,1)S(1)} collective-permute-done((bf16[320,4352]{1,0:T(8,128)(2,1)}, bf16[320,4352]{1,0:T(8,128)(2,1)S(1)}, u32[]{:S(2)}, u32[]{:S(2)}) %collective-permute-start) | collective-permute-done | bytes 2785312 | tf_op jit(solution)/shard_map/while/body/eval_jaxpr/ppermute | solution.py:10
  367.3 126.4 %all_to_all.5 = f32[16,320,320]{1,2,0:T(8,128)S(1)} all-to-all(f32[16,320,320]{1,2,0:T(8,128)} %get-tuple-element.184), channel_id=1, replica_groups=mesh['blk'=16,'freq'=8] {'blk'}, dimensions={0} | all-to-all | bytes 13107200 | tf_op jit(solution)/shard_map/all_to_all | solution.py:74
  493.7 7.2 %add.83 = f32[16,320,320]{1,2,0:T(8,128)} add(f32[16,320,320]{1,2,0:T(8,128)} %get-tuple-element.183, f32[16,320,320]{1,2,0:T(8,128)S(1)} %all_to_all.5) | non-fusion elementwise | flops 1638400 | bytes 19660800 | tf_op jit(solution)/shard_map/add | solution.py:75
  502.5 4.5 broadcast_in_dim.49
  507.0 5.1 fusion.3
  512.1 31.0 %psum.7 = f32[320,8]{0,1:T(8,128)S(1)} all-reduce(f32[320,8]{0,1:T(8,128)S(1)} %fusion.3), channel_id=1, replica_groups=mesh['blk'=16,'freq'=8] {'freq'}, use_global_device_ids=true, to_apply=%region_3.4 | all-reduce | flops 2560 | bytes 20480 | tf_op jit(solution)/shard_map/psum | solution.py:44
  543.2 59.4 %all-gather = f32[16,320,8]{1,2,0:T(8,128)S(1)} all-gather(f32[1,320,8]{1,2,0:T(8,128)S(1)} %bitcast.54), channel_id=1, replica_groups=mesh['blk'=16,'freq'=8] {'blk'}, dimensions={0}, use_global_device_ids=true | all-gather | bytes 174080 | tf_op jit(solution)/shard_map/all_gather | solution.py:45
  (71 shorter events, 91.6 us)
Async XLA Ops:
  6.5 1.3 copy-start
  6.5 3.7 copy-start.4
  6.5 596.6 %reduce-scatter.2.cloned.1.call-start = ((), (), s32[]{:S(2)}) async-start(), calls=%async_computation.2 | async-start | bytes 8847360 | tf_op jit(solution)/shard_map/reduce_scatter | solution.py:76
  20.5 5.6 copy-start.2
  29.3 3.1 copy-start.1
  32.4 34.4 %collective-permute-start = (bf16[320,4352]{1,0:T(8,128)(2,1)}, bf16[320,4352]{1,0:T(8,128)(2,1)S(1)}, u32[]{:S(2)}, u32[]{:S(2)}) collective-permute-start(bf16[320,4352]{1,0:T(8,128)(2,1)} %get-tuple-element.288), channel_id=1, source_target_pairs={{8,0},{16,8},{24,16},{32,24},{40,32},{48,40},{56,48},{64,56},{72,6... | collective-permute-start | bytes 8355848 | tf_op jit(solution)/shard_map/while/body/eval_jaxpr/ppermute | solution.py:10
  75.5 33.0 %collective-permute-start = (bf16[320,4352]{1,0:T(8,128)(2,1)}, bf16[320,4352]{1,0:T(8,128)(2,1)S(1)}, u32[]{:S(2)}, u32[]{:S(2)}) collective-permute-start(bf16[320,4352]{1,0:T(8,128)(2,1)} %get-tuple-element.288), channel_id=1, source_target_pairs={{8,0},{16,8},{24,16},{32,24},{40,32},{48,40},{56,48},{64,56},{72,6... | collective-permute-start | bytes 8355848 | tf_op jit(solution)/shard_map/while/body/eval_jaxpr/ppermute | solution.py:10
  117.2 33.0 %collective-permute-start = (bf16[320,4352]{1,0:T(8,128)(2,1)}, bf16[320,4352]{1,0:T(8,128)(2,1)S(1)}, u32[]{:S(2)}, u32[]{:S(2)}) collective-permute-start(bf16[320,4352]{1,0:T(8,128)(2,1)} %get-tuple-element.288), channel_id=1, source_target_pairs={{8,0},{16,8},{24,16},{32,24},{40,32},{48,40},{56,48},{64,56},{72,6... | collective-permute-start | bytes 8355848 | tf_op jit(solution)/shard_map/while/body/eval_jaxpr/ppermute | solution.py:10
  158.8 33.0 %collective-permute-start = (bf16[320,4352]{1,0:T(8,128)(2,1)}, bf16[320,4352]{1,0:T(8,128)(2,1)S(1)}, u32[]{:S(2)}, u32[]{:S(2)}) collective-permute-start(bf16[320,4352]{1,0:T(8,128)(2,1)} %get-tuple-element.288), channel_id=1, source_target_pairs={{8,0},{16,8},{24,16},{32,24},{40,32},{48,40},{56,48},{64,56},{72,6... | collective-permute-start | bytes 8355848 | tf_op jit(solution)/shard_map/while/body/eval_jaxpr/ppermute | solution.py:10
  200.6 33.0 %collective-permute-start = (bf16[320,4352]{1,0:T(8,128)(2,1)}, bf16[320,4352]{1,0:T(8,128)(2,1)S(1)}, u32[]{:S(2)}, u32[]{:S(2)}) collective-permute-start(bf16[320,4352]{1,0:T(8,128)(2,1)} %get-tuple-element.288), channel_id=1, source_target_pairs={{8,0},{16,8},{24,16},{32,24},{40,32},{48,40},{56,48},{64,56},{72,6... | collective-permute-start | bytes 8355848 | tf_op jit(solution)/shard_map/while/body/eval_jaxpr/ppermute | solution.py:10
  242.2 33.0 %collective-permute-start = (bf16[320,4352]{1,0:T(8,128)(2,1)}, bf16[320,4352]{1,0:T(8,128)(2,1)S(1)}, u32[]{:S(2)}, u32[]{:S(2)}) collective-permute-start(bf16[320,4352]{1,0:T(8,128)(2,1)} %get-tuple-element.288), channel_id=1, source_target_pairs={{8,0},{16,8},{24,16},{32,24},{40,32},{48,40},{56,48},{64,56},{72,6... | collective-permute-start | bytes 8355848 | tf_op jit(solution)/shard_map/while/body/eval_jaxpr/ppermute | solution.py:10
  283.9 33.0 %collective-permute-start = (bf16[320,4352]{1,0:T(8,128)(2,1)}, bf16[320,4352]{1,0:T(8,128)(2,1)S(1)}, u32[]{:S(2)}, u32[]{:S(2)}) collective-permute-start(bf16[320,4352]{1,0:T(8,128)(2,1)} %get-tuple-element.288), channel_id=1, source_target_pairs={{8,0},{16,8},{24,16},{32,24},{40,32},{48,40},{56,48},{64,56},{72,6... | collective-permute-start | bytes 8355848 | tf_op jit(solution)/shard_map/while/body/eval_jaxpr/ppermute | solution.py:10
  325.6 33.0 %collective-permute-start = (bf16[320,4352]{1,0:T(8,128)(2,1)}, bf16[320,4352]{1,0:T(8,128)(2,1)S(1)}, u32[]{:S(2)}, u32[]{:S(2)}) collective-permute-start(bf16[320,4352]{1,0:T(8,128)(2,1)} %get-tuple-element.288), channel_id=1, source_target_pairs={{8,0},{16,8},{24,16},{32,24},{40,32},{48,40},{56,48},{64,56},{72,6... | collective-permute-start | bytes 8355848 | tf_op jit(solution)/shard_map/while/body/eval_jaxpr/ppermute | solution.py:10
  501.0 6.1 copy-start.3
Sparse Core Ops, SparseCore 0:
  501.1 86.4 reduce-scatter.1
where the time goes:
time: 614 us; the launch traced here: 613 us
  blocking collectives  217 us (35%)
  waiting for transfers between devices  157 us (26%)
  starting transfers between devices  109 us (18%)
  local copies, waits for them, and re-layouts  52.9 us (9%)
  matrix products  49.6 us (8%)
  other arithmetic  14.7 us (2%)
  between operations  13.5 us (2%)
    ppermute x8, waiting for transfers between devices, passed_along(): return lax.ppermute(block, axis, route)  157 us
    all_to_all x1, blocking collectives, per_device(): lax.all_to_all(back_stack, 'blk', split_axis=0, concat_axis=0, tiled=True)  126 us
    ppermute x8, starting transfers between devices, passed_along(): return lax.ppermute(block, axis, route)  109 us
    all_gather x1, blocking collectives, per_device(): energy_all = lax.all_gather(energy_rows, 'blk', axis=0, tiled=True)  59.4 us
    dot_general x9, matrix products, record(): lax.dot_general(weighted, visitor, (((1,), (1,)), ((), ())), preferred_el...  36 us
    psum x1, blocking collectives, per_device(): energy_rows = lax.psum(partial_energy, 'freq')  31 us
    dynamic_update_slice x16, local copies, waits for them, and re-layouts, record(): own_stack = lax.dynamic_update_index_in_dim(own_stack, kept, slot_index, 0)  16.6 us
    while x8, local copies, waits for them, and re-layouts  12.5 us
  transfers between devices with their start and end apart: 9, of which 8 were waited for; matrix products, arithmetic and copies ran while one was open for 2% of the time, Pallas kernels for 0%

commit v1 on v0

v1 whole, which is shorter than its diff:
```python
import jax
import jax.numpy as jnp
from jax import lax
from jax.sharding import PartitionSpec as P

BOTH = ("blk", "freq")


def places():
    return [
        (yh, z, c, f) for yh in range(2) for z in range(4) for c in range(2) for f in range(8)
    ]


def place_index(yh, z, c, f):
    return (((yh % 2) * 4 + z % 4) * 2 + c % 2) * 8 + f % 8


def route(dyh, dz, dc):
    return [(place_index(yh, z, c, f), place_index(yh + dyh, z + dz, c + dc, f)) for yh, z, c, f in places()]


def send(block, dyh=0, dz=0, dc=0):
    return lax.ppermute(block, BOTH, route(dyh, dz, dc))


def per_device(spectra, labels, wedges, shells, shell_weight):
    rows, width = spectra.shape
    half = width // 2
    classes = wedges.shape[0]
    shell_count = shell_weight.shape[0]
    blk = lax.axis_index("blk")
    core, z, yh = blk % 2, (blk // 2) % 4, blk // 8
    freq = lax.axis_index("freq")
    first_core = core == 0
    class_range = jnp.arange(classes, dtype=jnp.int32)

    own_labels = lax.dynamic_slice_in_dim(labels, blk * rows, rows)
    own_hot = (own_labels[:, None] == class_range[None, :]).astype(jnp.bfloat16)
    wedge_pairs = jnp.repeat(wedges.astype(jnp.bfloat16), 2, axis=1)
    keep = jnp.dot(own_hot, wedge_pairs, preferred_element_type=jnp.float32)
    own = spectra * keep.astype(jnp.bfloat16)

    shell_hot = (shells[:, None] == jnp.arange(shell_count, dtype=jnp.int32)[None, :]).astype(jnp.float32)
    voxel_weight = jnp.dot(shell_hot, shell_weight, precision=lax.Precision.HIGHEST)
    weight = jnp.repeat(voxel_weight, 2)[None, :]

    def cols(block, which):
        return lax.dynamic_slice_in_dim(block, which * half, half, 1)

    high = z // 2
    next_high = ((z + 1) % 4) // 2
    sibling = send(own, dc=1)
    partner_a = send(cols(own, 1 - yh), dyh=1)
    following_c = send(own, dz=-1)
    previous_c = send(cols(own, next_high), dz=1)
    partner_b = send(cols(own, yh), dyh=1)
    partner_previous_c = send(partner_a, dz=1)
    partner_sibling = send(partner_a, dc=1)
    following_s = send(following_c, dc=1)
    previous_s = send(previous_c, dc=1)
    partner_previous_s = send(partner_previous_c, dc=1)

    squares = own.astype(jnp.float32) ** 2 * weight
    partial_energy = lax.dot_general(
        wedge_pairs.astype(jnp.float32), squares, (((1,), (1,)), ((), ())), precision=lax.Precision.HIGHEST
    )
    energy = lax.psum(partial_energy, "freq")
    energy_all = lax.all_gather(energy, "blk", axis=0, tiled=False)

    def scaled(block, weighted, scale):
        factor = jnp.where(weighted, scale, jnp.ones_like(scale))
        return (block.astype(jnp.float32) * factor).astype(jnp.bfloat16)

    def tile(a, b, on_b, scale):
        return lax.dot_general(
            scaled(a, jnp.logical_not(on_b), scale),
            scaled(b, on_b, scale),
            (((1,), (1,)), ((), ())),
            preferred_element_type=jnp.float32,
        )

    def in_order(mine, other, axis=0):
        return jnp.where(
            first_core,
            jnp.concatenate([mine, other], axis),
            jnp.concatenate([other, mine], axis),
        )

    def place(dyh, dz):
        return ((yh + dyh) % 2) * 4 + (z + dz) % 4

    def ahead(a, b):
        return (a - b) % 8 < 4

    scale_yh, scale_high = cols(weight, yh), cols(weight, high)
    partner_full = jnp.where(
        yh == 0,
        jnp.concatenate([partner_a, partner_b], 1),
        jnp.concatenate([partner_b, partner_a], 1),
    )
    following = in_order(following_c, following_s)
    lower_yh, lower_z = yh == 0, z < 2

    q1 = in_order(tile(own, own, False, weight), tile(sibling, own, first_core, weight))
    q2 = tile(following, own, ahead(place(0, 1), place(0, 0)), weight)
    q3 = tile(
        jnp.where(lower_z, cols(following, high), in_order(previous_c, previous_s)),
        jnp.where(lower_z, previous_c, cols(following_c, high)),
        jnp.where(lower_z, ahead(place(0, 1), place(0, -1)), ahead(place(0, -1), place(0, 1))),
        scale_high,
    )
    own_yh, sibling_yh = cols(own, yh), cols(sibling, yh)
    b4 = jnp.where(lower_yh, own_yh, partner_a)
    q4 = in_order(
        tile(jnp.where(lower_yh, partner_a, own_yh), b4, True, scale_yh),
        tile(
            jnp.where(lower_yh, partner_sibling, sibling_yh), b4, jnp.logical_not(first_core), scale_yh
        ),
    )
    q5 = tile(following, partner_full, ahead(place(0, 1), place(1, 0)), weight)
    q6 = tile(
        jnp.where(lower_yh, cols(following, yh), in_order(partner_previous_c, partner_previous_s)),
        jnp.where(lower_yh, partner_previous_c, cols(following_c, yh)),
        jnp.where(lower_yh, ahead(place(0, 1), place(1, -1)), ahead(place(1, -1), place(0, 1))),
        scale_yh,
    )
    slices = rows // 4

    def summed(tiles):
        stack = jnp.stack([t.reshape(8, slices, rows) for t in tiles], 1)
        return jnp.sum(lax.all_to_all(stack, "freq", 0, 0, tiled=True), 0)

    r1, r2, r3, r4, r5, r6 = summed([q1, q2, q3, q4, q5, q6])
    from_previous = send(jnp.stack([r2, r3, r5, r6]), dz=1)
    from_following = send(r3, dz=-1)
    from_partner = send(jnp.stack([r4, r5]), dyh=1)
    from_diagonal = send(r6, dyh=1, dz=-1)
    near = jnp.stack([r1, r2, from_previous[1] + from_following, from_previous[0]])
    far = jnp.stack([r4 + from_partner[0], from_partner[1], from_previous[3] + from_diagonal, from_previous[2]])
    near, far = (
        lax.dynamic_slice_in_dim(jnp.concatenate([part, part]), (4 - z) % 4, 4, 0) for part in (near, far)
    )
    pieces = jnp.where(lower_yh, jnp.concatenate([near, far]), jnp.concatenate([far, near]))
    found = lax.all_to_all(pieces, "freq", 0, 0, tiled=True).reshape(2 * rows, rows)
    swapped = send(lax.dynamic_slice_in_dim(found, (1 - core) * rows, rows, 0), dc=1)
    by_row = in_order(lax.dynamic_slice_in_dim(found, core * rows, rows, 0), swapped, 1)

    step_y, step_z = (freq // 4 + yh) % 2, (freq % 4 - z) % 4
    same_y = step_y == 0
    inner_z = jnp.logical_or(z == 1, z == 2)
    is_row = jnp.where(
        step_z == 0,
        jnp.logical_or(same_y, yh == 1),
        jnp.where(step_z == 1, False, jnp.where(step_z == 2, jnp.where(same_y, inner_z, yh == 0), True)),
    )
    products = jnp.where(is_row, by_row, found.T)

    column_labels = lax.dynamic_slice_in_dim(labels, freq * 2 * rows, 2 * rows)
    column_energy = lax.dynamic_slice_in_dim(energy_all, freq * 2, 2, 0)
    column_energy = jnp.concatenate([column_energy[0], column_energy[1]], 1)
    row_side = jnp.zeros_like(products)
    column_side = jnp.zeros_like(products)
    for d in range(classes):
        row_side = jnp.where(column_labels[None, :] == d, energy[d][:, None], row_side)
        column_side = jnp.where(own_labels[:, None] == d, column_energy[d][None, :], column_side)
    return products / jnp.sqrt(row_side * column_side + 1e-06)


def solution(mesh):
    placed = (P("blk", "freq"), P(), P(None, "freq"), P("freq"), P())
    return jax.shard_map(
        per_device, mesh=mesh, in_specs=placed, out_specs=P("blk", "freq"), check_vma=False
    )
```

time: 614 us -> 352 us (0.57)
  blocking collectives: 217 us -> 131 us
  starting transfers between devices: 109 us -> 27.7 us
  waiting for transfers between devices: 157 us -> 98 us
  local copies, waits for them, and re-layouts: 52.9 us -> 29.9 us
  between operations: 13.5 us -> 0.72 us
  other arithmetic: 14.7 us -> 25.1 us
  matrix products: 49.6 us -> 39.3 us
    ppermute x8 -> x15, starting transfers between devices: 109 us -> 23.5 us  [send(): return lax.ppermute(block, BOTH, route(dyh, dz, dc))]
    ppermute x8 -> x15, waiting for transfers between devices: 157 us -> 98 us  [send(): return lax.ppermute(block, BOTH, route(dyh, dz, dc))]
    all_to_all x1, blocking collectives: 126 us -> 72.4 us  [summed(): return jnp.sum(lax.all_to_all(stack, 'freq', 0, 0, tiled=True), 0)]
    all_gather x1, blocking collectives: 59.4 us -> 30.2 us  [per_device(): energy_all = lax.all_gather(energy, 'blk', axis=0, tiled=False)]
    dynamic_update_slice x17 -> x0, local copies, waits for them, and re-layouts: 16.7 us -> none  [the longest x16 16.6 us: record(): own_stack = lax.dynamic_update_index_in_dim(own_stack, kept, slot_index, 0)]
    while x8 -> x0, local copies, waits for them, and re-layouts: 12.5 us -> none
    dot_general x13 -> x10, matrix products: 48.1 us -> 38.5 us  [the longest x8 31.1 us: tile(): lax.dot_general(scaled(a, jnp.logical_not(on_b), scale), scaled(b, on_b,...]
    select_n x0 -> x6, other arithmetic: none -> 9.19 us  [the longest x3 7.96 us: in_order(): jnp.where(first_core, jnp.concatenate([mine, other], axis), jnp.concatena...]
  transfers between devices with their start and end apart: 9 -> 16, of which waited for: 8 -> 7; matrix products, arithmetic and copies ran while one was open for 2% -> 17% of each run, Pallas kernels for 0% -> 0%
where the time goes in v1:
time: 352 us; the launch traced here: 351 us
  blocking collectives  131 us (37%)
  waiting for transfers between devices  98 us (28%)
  matrix products  39.3 us (11%)
  local copies, waits for them, and re-layouts  29.9 us (8%)
  starting transfers between devices  27.7 us (8%)
  other arithmetic  25.1 us (7%)
    ppermute x15, waiting for transfers between devices, send(): return lax.ppermute(block, BOTH, route(dyh, dz, dc))  98 us
    all_to_all x1, blocking collectives, summed(): return jnp.sum(lax.all_to_all(stack, 'freq', 0, 0, tiled=True), 0)  72.4 us
    dot_general x8, matrix products, tile(): lax.dot_general(scaled(a, jnp.logical_not(on_b), scale), scaled(b, on_b,...  31.1 us
    all_gather x1, blocking collectives, per_device(): energy_all = lax.all_gather(energy, 'blk', axis=0, tiled=False)  30.2 us
    psum x1, blocking collectives, per_device(): energy = lax.psum(partial_energy, 'freq')  28 us
    ppermute x15, starting transfers between devices, send(): return lax.ppermute(block, BOTH, route(dyh, dz, dc))  23.5 us
    select_n x3, other arithmetic, in_order(): jnp.where(first_core, jnp.concatenate([mine, other], axis), jnp.concatena...  7.96 us
  transfers between devices with their start and end apart: 16, of which 7 were waited for; matrix products, arithmetic and copies ran while one was open for 17% of the time, Pallas kernels for 0%

profile of v1, /device:TPU:1, one launch (start us, length us, event | category | flops | bytes accessed | tf_op | source)
XLA Modules:
  0.0 351.3 jit_solution(6699036347489676391)
XLA Ops:
  2.0 5.8 %broadcast_in_dim.230 = bf16[8,2176,2]{0,2,1:T(2,128)(2,1)S(1)} broadcast(bf16[8,2176]{0,1:T(8,128)(2,1)S(1)} %copy.27), dimensions={0,1} | broadcast | bytes 104448 | tf_op jit(solution)/shard_map/broadcast_in_dim | solution.py:40
  7.8 3.1 fusion.2
  10.9 4.7 %collective-permute-start.1 = (bf16[320,4352]{1,0:T(8,128)(2,1)S(1)}, bf16[320,4352]{1,0:T(8,128)(2,1)}, u32[]{:S(2)}, u32[]{:S(2)}) collective-permute-start(bf16[320,4352]{1,0:T(8,128)(2,1)S(1)} %fusion.2), channel_id=1, source_target_pairs={{0,48},{1,49},{2,50},{3,51},{4,52},{5,53},{6,54},{7,55},{8,56},{9,... | collective-permute-start | bytes 8355848 | tf_op jit(solution)/shard_map/ppermute | solution.py:24
  21.6 53.1 %collective-permute-done.1 = bf16[320,4352]{1,0:T(8,128)(2,1)} collective-permute-done((bf16[320,4352]{1,0:T(8,128)(2,1)S(1)}, bf16[320,4352]{1,0:T(8,128)(2,1)}, u32[]{:S(2)}, u32[]{:S(2)}) %collective-permute-start.1) | collective-permute-done | bytes 2785312 | tf_op jit(solution)/shard_map/ppermute | solution.py:24
  86.4 3.5 fusion.60
  89.9 21.0 %collective-permute-done.3 = bf16[320,2176]{1,0:T(8,128)(2,1)} collective-permute-done((bf16[320,2176]{1,0:T(8,128)(2,1)}, bf16[320,2176]{1,0:T(8,128)(2,1)}, u32[]{:S(2)}, u32[]{:S(2)}) %collective-permute-start.3) | collective-permute-done | bytes 1392672 | tf_op jit(solution)/shard_map/ppermute | solution.py:24
  110.9 2.9 collective-permute-start.7
  114.9 3.4 fusion.19
  122.0 3.2 fusion.58
  128.9 11.9 %collective-permute-done.8 = bf16[320,2176]{1,0:T(8,128)(2,1)} collective-permute-done((bf16[320,2176]{1,0:T(8,128)(2,1)}, bf16[320,2176]{1,0:T(8,128)(2,1)}, u32[]{:S(2)}, u32[]{:S(2)}) %collective-permute-start.8) | collective-permute-done | bytes 1392672 | tf_op jit(solution)/shard_map/ppermute | solution.py:24
  142.6 5.5 %maximum_select_fusion = bf16[640,4352]{1,0:T(8,128)(2,1)S(1)} fusion(bf16[320,4352]{1,0:T(8,128)(2,1)} %collective-permute-done.2, bf16[320,4352]{1,0:T(8,128)(2,1)} %collective-permute-done.1, pred[]{:T(512)S(6)} %eq.214), kind=kLoop, calls=%fused_computation.17 | loop fusion | flops 25067520 | bytes 11141121 | tf_op jit(solution)/shard_map/jit(_where)/select_n | solution.py:84
  148.2 3.1 fusion.11
  151.3 5.8 %fusion.20 = f32[640,320]{1,0:T(8,128)S(1)} fusion(bf16[320,2176]{1,0:T(8,128)(2,1)} %collective-permute-done.4, bf16[320,2176]{1,0:T(8,128)(2,1)} %collective-permute-done.3, f32[2176]{0:T(1024)S(1)} %get-tuple-element.19, bf16[640,4352]{1,0:T(8,128)(2,1)S(1)} %maximum_select_fusion, s32[]{:T(128)S(6)} %select_n.516, pred[]{:T(512)S(6)} %eq.214, ...), kind=kOutput, calls=%fused_computation.30 | convolution fusion | flops 912179200 | bytes 9202176 | tf_op jit(solution)/shard_map/dot_general | solution.py:76
  157.3 5.8 %fusion.9 = f32[640,320]{1,0:T(8,128)S(1)} fusion(bf16[640,4352]{1,0:T(8,128)(2,1)S(1)} %maximum_select_fusion, f32[4352]{0:T(1024)S(1)} %get-tuple-element.55, bf16[320,2176]{1,0:T(8,128)(2,1)} %collective-permute-done.7, bf16[320,2176]{1,0:T(8,128)(2,1)} %collective-permute-done.5, f32[4352]{0:T(1024)S(1)} %get-tuple-element.54, pred[]{:T(512)S(6)} %eq.213), kind=kOutput, calls=%fused_computation.15 | convolution fusion | flops 1807646720 | bytes 9209857 | tf_op jit(solution)/shard_map/dot_general | solution.py:76
  163.1 4.8 %fusion.21 = f32[640,320]{1,0:T(8,128)S(1)} fusion(bf16[320,2176]{1,0:T(8,128)(2,1)S(1)} %collective-permute-done.9, bf16[320,2176]{1,0:T(8,128)(2,1)} %collective-permute-done.8, f32[2176]{0:T(1024)S(1)} %get-tuple-element.16, bf16[640,4352]{1,0:T(8,128)(2,1)S(1)} %maximum_select_fusion, s32[]{:T(128)S(6)} %select_n.535, pred[]{:T(512)S(6)} %eq.213, ...), kind=kOutput, calls=%fused_computation.31 | convolution fusion | flops 912179200 | bytes 9202176 | tf_op jit(solution)/shard_map/dot_general | solution.py:76
  168.5 72.4 %all_to_all.10 = f32[8,6,80,320]{3,2,1,0:T(8,128)} all-to-all(f32[8,6,80,320]{3,2,1,0:T(8,128)S(1)} %copy.34), channel_id=1, replica_groups=mesh['blk'=16,'freq'=8] {'freq'}, dimensions={0} | all-to-all | bytes 9830400 | tf_op jit(solution)/shard_map/all_to_all | solution.py:132
  241.0 3.1 reduce_sum.9
  251.2 7.5 %collective-permute-done.10 = f32[4,80,320]{2,1,0:T(8,128)} collective-permute-done((f32[4,80,320]{2,1,0:T(8,128)}, f32[4,80,320]{2,1,0:T(8,128)}, u32[]{:S(2)}, u32[]{:S(2)}) %collective-permute-start.10) | collective-permute-done | bytes 409632 | tf_op jit(solution)/shard_map/ppermute | solution.py:24
  266.3 3.3 collective-permute-done.12
  276.2 4.2 %all-to-all-start.1 = ((f32[8,80,320]{2,1,0:T(8,128)}), f32[8,80,320]{2,1,0:T(8,128)}, u32[]{:S(2)}, u32[]{:S(2)}) async-start(f32[8,80,320]{2,1,0:T(8,128)} %maximum_select_fusion.5), calls=%async_computation.1 | async-start | bytes 1966080 | tf_op jit(solution)/shard_map/all_to_all | solution.py:145
  280.6 4.3 %fusion.79 = f32[8,320]{1,0:T(8,128)S(1)} fusion(bf16[8,4352]{0,1:T(8,128)(2,1)} %bitcast.61, bf16[320,4352]{1,0:T(8,128)(2,1)S(1)} %fusion.2, f32[4352]{0:T(1024)S(1)} %mul.201), kind=kOutput, calls=%fused_computation.91 | convolution fusion | flops 137871360 | bytes 2882560 | tf_op jit(solution)/shard_map/dot_general | solution.py:65
  284.8 28.0 %psum.7 = f32[8,320]{1,0:T(8,128)S(1)} all-reduce(f32[8,320]{1,0:T(8,128)S(1)} %fusion.79), channel_id=1, replica_groups=mesh['blk'=16,'freq'=8] {'freq'}, use_global_device_ids=true, to_apply=%region_1.2 | all-reduce | flops 2560 | bytes 20480 | tf_op jit(solution)/shard_map/psum | solution.py:68
  312.8 30.2 %all-gather = f32[128,320]{1,0:T(8,128)S(1)} all-gather(f32[8,320]{1,0:T(8,128)S(1)} %psum.7), channel_id=2, replica_groups=mesh['blk'=16,'freq'=8] {'blk'}, dimensions={0}, use_global_device_ids=true | all-gather | bytes 174080 | tf_op jit(solution)/shard_map/all_gather | solution.py:69
  346.5 3.6 %fusion.84 = f32[320,640]{0,1:T(8,128)S(1)} fusion(f32[320,320]{0,1:T(8,128)S(1)} %collective-permute-done.14, f32[320,320]{0,1:T(8,128)S(1)} %copy.42, f32[8,80,320]{2,1,0:T(8,128)} %all-to-all-done.1, f32[640]{0:T(1024)S(1)} %get-tuple-element.11, f32[640]{0:T(1024)S(1)} %get-tuple-element.12, f32[640]{0:T(1024)S(1)} %get-tuple-element.10, ...), kind=kLoop, calls=%fused_computation.96 | loop fusion | flops 4710400 | bytes 2496002 | tf_op jit(solution)/shard_map/div | solution.py:167
  (84 shorter events, 56.4 us)
Async XLA Ops:
  0.0 76.6 %copy-start = (f32[28]{0:T(128)S(1)}, f32[28]{0:T(128)}, u32[]{:S(2)}) copy-start(f32[28]{0:T(128)} %param.9) | copy-start | bytes 340
  7.8 3.1 copy-start.2
  10.9 63.7 %collective-permute-start.1 = (bf16[320,4352]{1,0:T(8,128)(2,1)S(1)}, bf16[320,4352]{1,0:T(8,128)(2,1)}, u32[]{:S(2)}, u32[]{:S(2)}) collective-permute-start(bf16[320,4352]{1,0:T(8,128)(2,1)S(1)} %fusion.2), channel_id=1, source_target_pairs={{0,48},{1,49},{2,50},{3,51},{4,52},{5,53},{6,54},{7,55},{8,56},{9,... | collective-permute-start | bytes 8355848 | tf_op jit(solution)/shard_map/ppermute | solution.py:24
  15.6 98.2 %collective-permute-start = (bf16[320,4352]{1,0:T(8,128)(2,1)S(1)}, bf16[320,4352]{1,0:T(8,128)(2,1)}, u32[]{:S(2)}, u32[]{:S(2)}) collective-permute-start(bf16[320,4352]{1,0:T(8,128)(2,1)S(1)} %fusion.2), channel_id=1, source_target_pairs={{0,8},{1,9},{2,10},{3,11},{4,12},{5,13},{6,14},{7,15},{8,0},{9,1},... | collective-permute-start | bytes 8355848 | tf_op jit(solution)/shard_map/ppermute | solution.py:24
  16.6 60.0 %copy-start.5 = (s32[2176]{0:T(1024)S(1)}, s32[2176]{0:T(1024)}, u32[]{:S(2)}) copy-start(s32[2176]{0:T(1024)} %param.8) | copy-start | bytes 26116
  18.7 61.8 %collective-permute-start.5 = (bf16[320,2176]{1,0:T(8,128)(2,1)}, bf16[320,2176]{1,0:T(8,128)(2,1)}, u32[]{:S(2)}, u32[]{:S(2)}) collective-permute-start(bf16[320,2176]{1,0:T(8,128)(2,1)} %get-tuple-element.31), channel_id=1, source_target_pairs={{0,64},{1,65},{2,66},{3,67},{4,68},{5,69},{6,70},{7,71},{8,72},{9,... | collective-permute-start | bytes 4177928 | tf_op jit(solution)/shard_map/ppermute | solution.py:24
  74.6 68.0 %collective-permute-start.2 = (bf16[320,4352]{1,0:T(8,128)(2,1)}, bf16[320,4352]{1,0:T(8,128)(2,1)}, u32[]{:S(2)}, u32[]{:S(2)}) collective-permute-start(bf16[320,4352]{1,0:T(8,128)(2,1)} %collective-permute-done.1), channel_id=1, source_target_pairs={{0,8},{1,9},{2,10},{3,11},{4,12},{5,13},{6,14},{7,15},{8,0},{9,1},... | collective-permute-start | bytes 8355848 | tf_op jit(solution)/shard_map/ppermute | solution.py:24
  76.2 34.7 %collective-permute-start.3 = (bf16[320,2176]{1,0:T(8,128)(2,1)}, bf16[320,2176]{1,0:T(8,128)(2,1)}, u32[]{:S(2)}, u32[]{:S(2)}) collective-permute-start(bf16[320,2176]{1,0:T(8,128)(2,1)} %get-tuple-element.32), channel_id=1, source_target_pairs={{0,16},{1,17},{2,18},{3,19},{4,20},{5,21},{6,22},{7,23},{8,24},{9,... | collective-permute-start | bytes 4177928 | tf_op jit(solution)/shard_map/ppermute | solution.py:24
  80.5 41.5 %collective-permute-start.6 = (bf16[320,2176]{1,0:T(8,128)(2,1)}, bf16[320,2176]{1,0:T(8,128)(2,1)}, u32[]{:S(2)}, u32[]{:S(2)}) collective-permute-start(bf16[320,2176]{1,0:T(8,128)(2,1)} %collective-permute-done.5), channel_id=1, source_target_pairs={{0,8},{1,9},{2,10},{3,11},{4,12},{5,13},{6,14},{7,15},{8,0},{9,1},... | collective-permute-start | bytes 4177928 | tf_op jit(solution)/shard_map/ppermute | solution.py:24
  84.9 55.9 %collective-permute-start.8 = (bf16[320,2176]{1,0:T(8,128)(2,1)}, bf16[320,2176]{1,0:T(8,128)(2,1)}, u32[]{:S(2)}, u32[]{:S(2)}) collective-permute-start(bf16[320,2176]{1,0:T(8,128)(2,1)} %collective-permute-done.5), channel_id=1, source_target_pairs={{0,16},{1,17},{2,18},{3,19},{4,20},{5,21},{6,22},{7,23},{8,24},{9,... | collective-permute-start | bytes 4177928 | tf_op jit(solution)/shard_map/ppermute | solution.py:24
  110.9 46.3 %collective-permute-start.7 = (bf16[320,2176]{1,0:T(8,128)(2,1)}, bf16[320,2176]{1,0:T(8,128)(2,1)}, u32[]{:S(2)}, u32[]{:S(2)}) collective-permute-start(bf16[320,2176]{1,0:T(8,128)(2,1)} %get-tuple-element.30), channel_id=1, source_target_pairs={{0,64},{1,65},{2,66},{3,67},{4,68},{5,69},{6,70},{7,71},{8,72},{9,... | collective-permute-start | bytes 4177928 | tf_op jit(solution)/shard_map/ppermute | solution.py:24
  113.8 37.5 %collective-permute-start.4 = (bf16[320,2176]{1,0:T(8,128)(2,1)}, bf16[320,2176]{1,0:T(8,128)(2,1)}, u32[]{:S(2)}, u32[]{:S(2)}) collective-permute-start(bf16[320,2176]{1,0:T(8,128)(2,1)} %collective-permute-done.3), channel_id=1, source_target_pairs={{0,8},{1,9},{2,10},{3,11},{4,12},{5,13},{6,14},{7,15},{8,0},{9,1},... | collective-permute-start | bytes 4177928 | tf_op jit(solution)/shard_map/ppermute | solution.py:24
  122.0 3.3 copy-start.4
  140.8 22.4 %collective-permute-start.9 = (bf16[320,2176]{1,0:T(8,128)(2,1)}, bf16[320,2176]{1,0:T(8,128)(2,1)S(1)}, u32[]{:S(2)}, u32[]{:S(2)}) collective-permute-start(bf16[320,2176]{1,0:T(8,128)(2,1)} %collective-permute-done.8), channel_id=1, source_target_pairs={{0,8},{1,9},{2,10},{3,11},{4,12},{5,13},{6,14},{7,15},{8,0},{9,1},... | collective-permute-start | bytes 4177928 | tf_op jit(solution)/shard_map/ppermute | solution.py:24
  151.3 5.9 %copy-start.3 = (f32[640,320]{1,0:T(8,128)S(1)}, f32[640,320]{1,0:T(8,128)}, u32[]{:S(2)}) copy-start(f32[640,320]{1,0:T(8,128)} %copy.31) | copy-start | bytes 2457604
  245.6 13.1 %collective-permute-start.10 = (f32[4,80,320]{2,1,0:T(8,128)}, f32[4,80,320]{2,1,0:T(8,128)}, u32[]{:S(2)}, u32[]{:S(2)}) collective-permute-start(f32[4,80,320]{2,1,0:T(8,128)} %pad_maximum_fusion), channel_id=1, source_target_pairs={{0,16},{1,17},{2,18},{3,19},{4,20},{5,21},{6,22},{7,23},{8,24},{9,... | collective-permute-start | bytes 1228808 | tf_op jit(solution)/shard_map/ppermute | solution.py:24
  246.4 4.9 %collective-permute-start.11 = (f32[80,320]{1,0:T(8,128)}, f32[80,320]{1,0:T(8,128)}, u32[]{:S(2)}, u32[]{:S(2)}) collective-permute-start(f32[80,320]{1,0:T(8,128)} %get-tuple-element.37), channel_id=1, source_target_pairs={{0,48},{1,49},{2,50},{3,51},{4,52},{5,53},{6,54},{7,55},{8,56},{9,... | collective-permute-start | bytes 307208 | tf_op jit(solution)/shard_map/ppermute | solution.py:24
  249.0 20.6 %collective-permute-start.13 = (f32[80,320]{1,0:T(8,128)}, f32[80,320]{1,0:T(8,128)S(1)}, u32[]{:S(2)}, u32[]{:S(2)}) collective-permute-start(f32[80,320]{1,0:T(8,128)} %get-tuple-element.38), channel_id=1, source_target_pairs={{0,112},{1,113},{2,114},{3,115},{4,116},{5,117},{6,118},{7,119},{8... | collective-permute-start | bytes 307208 | tf_op jit(solution)/shard_map/ppermute | solution.py:24
  262.7 6.9 %collective-permute-start.12 = (f32[2,80,320]{2,1,0:T(8,128)S(1)}, f32[2,80,320]{2,1,0:T(8,128)S(1)}, u32[]{:S(2)}, u32[]{:S(2)}) collective-permute-start(f32[2,80,320]{2,1,0:T(8,128)S(1)} %get-tuple-element.36), channel_id=1, source_target_pairs={{0,64},{1,65},{2,66},{3,67},{4,68},{5,69},{6,70},{7,71},{8,72},{9,... | collective-permute-start | bytes 614408 | tf_op jit(solution)/shard_map/ppermute | solution.py:24
  276.2 66.9 %all-to-all-start.1 = ((f32[8,80,320]{2,1,0:T(8,128)}), f32[8,80,320]{2,1,0:T(8,128)}, u32[]{:S(2)}, u32[]{:S(2)}) async-start(f32[8,80,320]{2,1,0:T(8,128)} %maximum_select_fusion.5), calls=%async_computation.1 | async-start | bytes 1966080 | tf_op jit(solution)/shard_map/all_to_all | solution.py:145
  344.6 1.9 collective-permute-start.14
  345.7 5.7 %copy-start.1 = (f32[28]{0:T(128)S(1)}, f32[28]{0:T(128)}, u32[]{:S(2)}) copy-start(f32[28]{0:T(128)} %param.9) | copy-start | bytes 340

commit v2 on v0

v2 whole, which is shorter than its diff:
```python
import jax
import jax.numpy as jnp
from jax import lax
from jax.experimental import pallas as pl
from jax.experimental.pallas import tpu as pltpu
from jax.sharding import PartitionSpec as P

BOTH = ("blk", "freq")
VMEM_BYTES = 60 * 1024 * 1024
LANES = 128


def places():
    return [
        (yh, z, c, f) for yh in range(2) for z in range(4) for c in range(2) for f in range(8)
    ]


def place_index(yh, z, c, f):
    return (((yh % 2) * 4 + z % 4) * 2 + c % 2) * 8 + f % 8


def route(dyh, dz, dc):
    return [(place_index(yh, z, c, f), place_index(yh + dyh, z + dz, c + dc, f)) for yh, z, c, f in places()]


def send(block, dyh=0, dz=0, dc=0):
    return lax.ppermute(block, BOTH, route(dyh, dz, dc))


def together(*arrays):
    return lax.optimization_barrier(arrays)


def scaled(block, weighted, weight):
    factor = jnp.where(jnp.full(weight.shape, weighted, jnp.int32) > 0, weight, 1.0)
    return (block.astype(jnp.float32) * factor).astype(jnp.bfloat16)


def gram(a, b):
    return lax.dot_general(a, b, (((1,), (1,)), ((), ())), preferred_element_type=jnp.float32)


CORE, YH, LOW, HIGH, NEXT_HIGH, ON_B2, ON_B3, ON_B5, ON_B6, Z = range(10)


def mask_kernel(info, shell_weight, hot, spectra, wedges, shells, own, to_partner, to_next, pairs, weight):
    half = spectra.shape[1] // 2
    step = 2 * LANES

    @pl.when(pl.program_id(0) == 0)
    def _():
        place = lax.broadcasted_iota(jnp.int32, (LANES, step), 0)
        spread = (lax.broadcasted_iota(jnp.int32, (LANES, step), 1) // 2 == place).astype(jnp.bfloat16)

        def widen(x):
            return jnp.dot(x, spread, preferred_element_type=jnp.float32)

        for j in range(spectra.shape[1] // step):
            some, wide = pl.ds(j * LANES, LANES), pl.ds(j * step, step)
            pairs[:, wide] = widen(wedges[:, some].astype(jnp.float32).astype(jnp.bfloat16)).astype(jnp.bfloat16)
            shell = shells[:, some]
            value = jnp.zeros(shell.shape, jnp.float32)
            for k in range(shell_weight.shape[0]):
                value = jnp.where(shell == k, shell_weight[k], value)
            top = value.astype(jnp.bfloat16)
            rest = value - top.astype(jnp.float32)
            middle = rest.astype(jnp.bfloat16)
            low = (rest - middle.astype(jnp.float32)).astype(jnp.bfloat16)
            weight[:, wide] = (widen(top) + widen(middle)) + widen(low)

    keep = jnp.dot(hot[...], pairs[...], preferred_element_type=jnp.float32).astype(jnp.bfloat16)
    own[...] = spectra[...] * keep
    to_partner[...] = own[:, pl.ds(pl.multiple_of((1 - info[YH]) * half, LANES), half)]
    to_next[...] = own[:, pl.ds(pl.multiple_of(info[NEXT_HIGH] * half, LANES), half)]


def masked_blocks(info, shell_weight, hot, spectra, wedges, shells):
    rows, width = spectra.shape
    classes = wedges.shape[0]
    part = rows // 4
    whole = lambda *shape: pl.BlockSpec(shape, lambda i, info: (0, 0))
    slab = lambda n: pl.BlockSpec((part, n), lambda i, info: (i, 0))
    return pl.pallas_call(
        mask_kernel,
        grid_spec=pltpu.PrefetchScalarGridSpec(
            num_scalar_prefetch=1,
            grid=(4,),
            in_specs=[
                pl.BlockSpec(memory_space=pltpu.SMEM),
                slab(classes),
                slab(width),
                whole(classes, width // 2),
                whole(1, width // 2),
            ],
            out_specs=[slab(width), slab(width // 2), slab(width // 2), whole(classes, width), whole(1, width)],
        ),
        out_shape=[
            jax.ShapeDtypeStruct((rows, width), jnp.bfloat16),
            jax.ShapeDtypeStruct((rows, width // 2), jnp.bfloat16),
            jax.ShapeDtypeStruct((rows, width // 2), jnp.bfloat16),
            jax.ShapeDtypeStruct((classes, width), jnp.bfloat16),
            jax.ShapeDtypeStruct((1, width), jnp.float32),
        ],
        compiler_params=pltpu.CompilerParams(vmem_limit_bytes=VMEM_BYTES),
    )(info, shell_weight, hot, spectra, wedges, shells)


def mine(i):
    return jnp.minimum(i, 1)


def others(i):
    return jnp.maximum(i - 2, 0)


def rank(i, info):
    return jnp.where(i < 2, info[CORE], 1 - info[CORE]) * 2 + i % 2


def first_kernel(info, a_mine, a_other, b, weight, out):
    i = pl.program_id(0)
    w = weight[...]
    slices = out.shape[1]

    def product(a, on_b):
        tile = gram(scaled(a[...], 1 - on_b, w), scaled(b[...], on_b, w))
        out[...] = tile.reshape(2, slices, tile.shape[1])

    @pl.when(i < 2)
    def _():
        product(a_mine, 0)

    @pl.when(i >= 2)
    def _():
        product(a_other, 1 - info[CORE])


def first_tiles(info, own, sibling, weight):
    rows, width = own.shape
    part = rows // 2
    return pl.pallas_call(
        first_kernel,
        grid_spec=pltpu.PrefetchScalarGridSpec(
            num_scalar_prefetch=1,
            grid=(4,),
            in_specs=[
                pl.BlockSpec((part, width), lambda i, info: (mine(i), 0)),
                pl.BlockSpec((part, width), lambda i, info: (others(i), 0)),
                pl.BlockSpec((rows, width), lambda i, info: (0, 0)),
                pl.BlockSpec((1, width), lambda i, info: (0, 0)),
            ],
            out_specs=pl.BlockSpec((2, part // 2, rows), lambda i, info: (rank(i, info), 0, 0)),
        ),
        out_shape=jax.ShapeDtypeStruct((8, part // 2, rows), jnp.float32),
        compiler_params=pltpu.CompilerParams(vmem_limit_bytes=VMEM_BYTES),
    )(info, own, sibling, own, weight)


def fourth_kernel(info, own, own_a, sibling_a, partner, partner_a, partner_sibling_a, weight, out):
    i = pl.program_id(0)
    w = weight[...]
    slices = out.shape[1]

    def product(a, b, on_b):
        tile = gram(scaled(a[...], 1 - on_b, w), scaled(b[...], on_b, w))
        out[...] = tile.reshape(2, slices, tile.shape[1])

    lower = info[YH] == 0
    for is_mine, is_lower, a, b in (
        (True, True, partner_a, own),
        (True, False, own_a, partner),
        (False, True, partner_sibling_a, own),
        (False, False, sibling_a, partner),
    ):

        @pl.when(jnp.logical_and((i < 2) == is_mine, lower == is_lower))
        def _(a=a, b=b, on_b=1 if is_mine else info[CORE]):
            product(a, b, on_b)


def fourth_tiles(info, own, sibling, partner, partner_sibling, weight):
    rows, half = partner.shape
    part = rows // 2
    return pl.pallas_call(
        fourth_kernel,
        grid_spec=pltpu.PrefetchScalarGridSpec(
            num_scalar_prefetch=1,
            grid=(4,),
            in_specs=[
                pl.BlockSpec((rows, half), lambda i, info: (0, info[YH])),
                pl.BlockSpec((part, half), lambda i, info: (mine(i), info[YH])),
                pl.BlockSpec((part, half), lambda i, info: (others(i), info[YH])),
                pl.BlockSpec((rows, half), lambda i, info: (0, 0)),
                pl.BlockSpec((part, half), lambda i, info: (mine(i), 0)),
                pl.BlockSpec((part, half), lambda i, info: (others(i), 0)),
                pl.BlockSpec((1, half), lambda i, info: (0, info[YH])),
            ],
            out_specs=pl.BlockSpec((2, part // 2, rows), lambda i, info: (rank(i, info), 0, 0)),
        ),
        out_shape=jax.ShapeDtypeStruct((8, part // 2, rows), jnp.float32),
        compiler_params=pltpu.CompilerParams(vmem_limit_bytes=VMEM_BYTES),
    )(info, own, own, sibling, partner, partner, partner_sibling, weight)


def late_kernel(
    info, own, near_half, far_half, previous, diagonal, following_high, following_yh, a_mine, a_other,
    previous_mine, previous_other, diagonal_mine, diagonal_other, weight, out, own_b, partner_b, third_b, sixth_b,
):
    i = pl.program_id(0)
    half = previous.shape[1]
    slices = out.shape[2]
    lower, low = info[YH] == 0, info[LOW] == 1

    def span(which):
        return pl.ds(pl.multiple_of(which * half, LANES), half)

    at_yh, at_other, at_high = span(info[YH]), span(1 - info[YH]), span(info[HIGH])

    @pl.when(i == 0)
    def _():
        own_b[...] = scaled(own[...], info[ON_B2], weight[...])
        partner_b[:, at_yh] = scaled(near_half[...], info[ON_B5], weight[:, at_yh])
        partner_b[:, at_other] = scaled(far_half[...], info[ON_B5], weight[:, at_other])

        @pl.when(low)
        def _():
            third_b[...] = scaled(previous[...], info[ON_B3], weight[:, at_high])

        @pl.when(jnp.logical_not(low))
        def _():
            third_b[...] = scaled(following_high[...], info[ON_B3], weight[:, at_high])

        @pl.when(lower)
        def _():
            sixth_b[...] = scaled(diagonal[...], info[ON_B6], weight[:, at_yh])

        @pl.when(jnp.logical_not(lower))
        def _():
            sixth_b[...] = scaled(following_yh[...], info[ON_B6], weight[:, at_yh])

    def put(k, a, on_b, w, b):
        tile = gram(scaled(a, 1 - on_b, w), b[...])
        out[:, k] = tile.reshape(2, slices, tile.shape[1])

    def products(a, earlier, across):
        put(0, a[...], info[ON_B2], weight[...], own_b)
        put(2, a[...], info[ON_B5], weight[...], partner_b)

        @pl.when(low)
        def _():
            put(1, a[:, at_high], info[ON_B3], weight[:, at_high], third_b)

        @pl.when(jnp.logical_not(low))
        def _():
            put(1, earlier[...], info[ON_B3], weight[:, at_high], third_b)

        @pl.when(lower)
        def _():
            put(3, a[:, at_yh], info[ON_B6], weight[:, at_yh], sixth_b)

        @pl.when(jnp.logical_not(lower))
        def _():
            put(3, across[...], info[ON_B6], weight[:, at_yh], sixth_b)

    @pl.when(i < 2)
    def _():
        products(a_mine, previous_mine, diagonal_mine)

    @pl.when(i >= 2)
    def _():
        products(a_other, previous_other, diagonal_other)


def late_tiles(info, own, near_half, far_half, previous, previous_s, diagonal, diagonal_s, following, following_s, weight):
    rows, width = own.shape
    half, part = width // 2, rows // 2
    full = lambda n, at=lambda info: 0: pl.BlockSpec((rows, n), lambda i, info: (0, at(info)))
    slab = lambda n, which: pl.BlockSpec((part, n), lambda i, info: (which(i), 0))
    return pl.pallas_call(
        late_kernel,
        grid_spec=pltpu.PrefetchScalarGridSpec(
            num_scalar_prefetch=1,
            grid=(4,),
            in_specs=[
                full(width),
                full(half),
                full(half),
                full(half),
                full(half),
                full(half, lambda info: info[HIGH]),
                full(half, lambda info: info[YH]),
                slab(width, mine),
                slab(width, others),
                slab(half, mine),
                slab(half, others),
                slab(half, mine),
                slab(half, others),
                pl.BlockSpec((1, width), lambda i, info: (0, 0)),
            ],
            out_specs=pl.BlockSpec((2, 4, part // 2, rows), lambda i, info: (rank(i, info), 0, 0, 0)),
            scratch_shapes=[
                pltpu.VMEM((rows, width), jnp.bfloat16),
                pltpu.VMEM((rows, width), jnp.bfloat16),
                pltpu.VMEM((rows, half), jnp.bfloat16),
                pltpu.VMEM((rows, half), jnp.bfloat16),
            ],
        ),
        out_shape=jax.ShapeDtypeStruct((8, 4, part // 2, rows), jnp.float32),
        compiler_params=pltpu.CompilerParams(vmem_limit_bytes=VMEM_BYTES),
    )(
        info, own, near_half, far_half, previous, diagonal, following, following, following, following_s,
        previous, previous_s, diagonal, diagonal_s, weight,
    )


def gather_kernel(info, r1, r2, r4, from_previous, from_following, from_partner, from_diagonal, out):
    yh, z = info[YH], info[Z]

    def put(dyh, dz, value):
        out[(yh + dyh) % 2 * 4 + (z + dz) % 4] = value

    put(0, 0, r1[...])
    put(0, 1, r2[...])
    put(0, 2, from_previous[1] + from_following[...])
    put(0, 3, from_previous[0])
    put(1, 0, r4[...] + from_partner[0])
    put(1, 1, from_partner[1])
    put(1, 2, from_previous[3] + from_diagonal[...])
    put(1, 3, from_previous[2])


def gathered(info, *parts):
    slices, rows = parts[0].shape
    vmem = pl.BlockSpec(memory_space=pltpu.VMEM)
    return pl.pallas_call(
        gather_kernel,
        in_specs=[pl.BlockSpec(memory_space=pltpu.SMEM)] + [vmem] * len(parts),
        out_specs=vmem,
        out_shape=jax.ShapeDtypeStruct((8, slices, rows), jnp.float32),
    )(info, *parts)


def final_kernel(info, found, swapped, root, out):
    rows = swapped.shape[0]
    core, by_row = info[0], info[1]

    for is_first in (True, False):

        @pl.when(jnp.logical_and(by_row == 1, (core == 0) == is_first))
        def _(is_first=is_first):
            kept = found[:rows] if is_first else found[rows:]
            pair = (kept, swapped[...]) if is_first else (swapped[...], kept)
            out[...] = jnp.concatenate(pair, 1) / root[...]

    @pl.when(by_row == 0)
    def _():
        out[...] = found[...].T / root[...]


def finished(info, found, swapped, root):
    vmem = pl.BlockSpec(memory_space=pltpu.VMEM)
    return pl.pallas_call(
        final_kernel,
        in_specs=[pl.BlockSpec(memory_space=pltpu.SMEM), vmem, vmem, vmem],
        out_specs=vmem,
        out_shape=jax.ShapeDtypeStruct(root.shape, jnp.float32),
    )(info, found, swapped, root)


def per_device(spectra, labels, wedges, shells, shell_weight):
    rows, width = spectra.shape
    half = width // 2
    classes = wedges.shape[0]
    blk = lax.axis_index("blk")
    core, z, yh = blk % 2, (blk // 2) % 4, blk // 8
    freq = lax.axis_index("freq")

    def place(dyh, dz):
        return ((yh + dyh) % 2) * 4 + (z + dz) % 4

    def ahead(a, b):
        return ((a - b) % 8 < 4).astype(jnp.int32)

    low, lower = z < 2, yh == 0
    info = jnp.stack(
        [
            core,
            yh,
            low.astype(jnp.int32),
            z // 2,
            ((z + 1) % 4) // 2,
            ahead(place(0, 1), place(0, 0)),
            jnp.where(low, ahead(place(0, 1), place(0, -1)), ahead(place(0, -1), place(0, 1))),
            ahead(place(0, 1), place(1, 0)),
            jnp.where(lower, ahead(place(0, 1), place(1, -1)), ahead(place(1, -1), place(0, 1))),
            z,
        ]
    ).astype(jnp.int32)

    class_range = jnp.arange(classes, dtype=jnp.int32)
    own_labels = lax.dynamic_slice_in_dim(labels, blk * rows, rows)
    hot = (own_labels[:, None] == class_range[None, :]).astype(jnp.bfloat16)
    own, to_partner, to_next, pairs, weight = masked_blocks(info, shell_weight, hot, spectra, wedges, shells[None, :])

    following = send(own, dz=-1)
    partner_a = send(to_partner, dyh=1)
    previous = send(to_next, dz=1)
    sibling = send(own, dc=1)

    squares = own.astype(jnp.float32) ** 2 * weight
    partial_energy = lax.dot_general(
        pairs.astype(jnp.float32), squares, (((1,), (1,)), ((), ())), precision=lax.Precision.HIGHEST
    )
    q1 = first_tiles(info, own, sibling, weight)
    q1 = jnp.concatenate([q1, jnp.broadcast_to(partial_energy[None], (8, classes, rows))], 1)
    r1 = jnp.sum(lax.all_to_all(q1, "freq", 0, 0, tiled=True), 0)
    energy, r1 = r1[rows // 4 :], r1[: rows // 4]
    to_partner_b = lax.dynamic_slice_in_dim(own, yh * half, half, 1)
    partner_a, previous, to_partner_b, r1, energy = together(partner_a, previous, to_partner_b, r1, energy)

    partner_b = send(to_partner_b, dyh=1)
    diagonal = send(partner_a, dz=1)
    partner_sibling = send(partner_a, dc=1)
    previous_s = send(previous, dc=1)
    q4 = fourth_tiles(info, own, sibling, partner_a, partner_sibling, weight)
    r4 = jnp.sum(lax.all_to_all(q4, "freq", 0, 0, tiled=True), 0)
    energy_all = lax.all_to_all(jnp.broadcast_to(energy[None], (16, classes, rows)), "blk", 0, 0, tiled=True)
    column_labels = lax.dynamic_slice_in_dim(labels, freq * 2 * rows, 2 * rows)
    column_energy = lax.dynamic_slice_in_dim(energy_all, freq * 2, 2, 0)
    column_energy = jnp.concatenate([column_energy[0], column_energy[1]], 1)
    row_side = jnp.zeros((rows, 2 * rows), jnp.float32)
    column_side = jnp.zeros((rows, 2 * rows), jnp.float32)
    for d in range(classes):
        row_side = jnp.where(column_labels[None, :] == d, energy[d][:, None], row_side)
        column_side = jnp.where(own_labels[:, None] == d, column_energy[d][None, :], column_side)
    root = jnp.sqrt(row_side * column_side + 1e-06)
    following, diagonal, partner_b, r4, root = together(following, diagonal, partner_b, r4, root)

    following_s = send(following, dc=1)
    diagonal_s = send(diagonal, dc=1)
    late = late_tiles(
        info, own, partner_a, partner_b, previous, previous_s, diagonal, diagonal_s, following, following_s, weight
    )
    late = jnp.sum(lax.all_to_all(late, "freq", 0, 0, tiled=True), 0)

    from_previous = send(late, dz=1)
    from_following = send(late[1], dz=-1)
    from_partner = send(jnp.stack([r4, late[2]]), dyh=1)
    from_diagonal = send(late[3], dyh=1, dz=-1)
    from_previous, from_following, from_partner, from_diagonal = together(
        from_previous, from_following, from_partner, from_diagonal
    )
    pieces = gathered(info, r1, late[0], r4, from_previous, from_following, from_partner, from_diagonal)
    found = lax.all_to_all(pieces, "freq", 0, 0, tiled=True).reshape(2 * rows, rows)
    swapped = send(lax.dynamic_slice_in_dim(found, (1 - core) * rows, rows, 0), dc=1)

    step_y, step_z = (freq // 4 + yh) % 2, (freq % 4 - z) % 4
    same_y = step_y == 0
    inner_z = jnp.logical_or(z == 1, z == 2)
    by_row = jnp.where(
        step_z == 0,
        jnp.logical_or(same_y, yh == 1),
        jnp.where(step_z == 1, False, jnp.where(step_z == 2, jnp.where(same_y, inner_z, lower), True)),
    )
    return finished(jnp.stack([core, by_row.astype(jnp.int32)]), found, swapped, root)


def solution(mesh):
    placed = (P("blk", "freq"), P(), P(None, "freq"), P("freq"), P())
    return jax.shard_map(
        per_device, mesh=mesh, in_specs=placed, out_specs=P("blk", "freq"), check_vma=False
    )
```

time: 614 us -> 258 us (0.42)
  blocking collectives: 217 us -> 51.2 us
  waiting for transfers between devices: 157 us -> 80.1 us
  starting transfers between devices: 109 us -> 41.6 us
  Pallas kernels: 0 us -> 52.7 us
  matrix products: 49.6 us -> 4.71 us
  local copies, waits for them, and re-layouts: 52.9 us -> 12.1 us
  between operations: 13.5 us -> 0.19 us
    ppermute x8 -> x15, waiting for transfers between devices: 157 us -> 14.1 us  [send(): return lax.ppermute(block, BOTH, route(dyh, dz, dc))]
    ppermute x8 -> x15, starting transfers between devices: 109 us -> 22.2 us  [send(): return lax.ppermute(block, BOTH, route(dyh, dz, dc))]
    all_to_all x1, blocking collectives: 126 us -> 51.2 us  [per_device(): late = jnp.sum(lax.all_to_all(late, 'freq', 0, 0, tiled=True), 0)]
    all_to_all x0 -> x4, waiting for transfers between devices: none -> 66 us  [the longest x1 24.2 us: per_device(): lax.all_to_all(jnp.broadcast_to(energy[None], (16, classes, rows)), 'blk'...]
    all_gather x1 -> x0, blocking collectives: 59.4 us -> none  [per_device(): energy_all = lax.all_gather(energy_rows, 'blk', axis=0, tiled=True)]
    pallas_call x0 -> x6, Pallas kernels: none -> 52.7 us  [the longest x1 23.7 us: late_tiles(): pl.pallas_call(late_kernel, grid_spec=pltpu.PrefetchScalarGridSpec(num_sc...]
    dot_general x14 -> x1, matrix products: 49.6 us -> 4.71 us  [per_device(): lax.dot_general(pairs.astype(jnp.float32), squares, (((1,), (1,)), ((), (...]
    psum x1 -> x0, blocking collectives: 31 us -> none  [per_device(): energy_rows = lax.psum(partial_energy, 'freq')]
  transfers between devices with their start and end apart: 9 -> 19, of which waited for: 8 -> 9; matrix products, arithmetic and copies ran while one was open for 2% -> 7% of each run, Pallas kernels for 0% -> 7%
where the time goes in v2:
time: 258 us; the launch traced here: 257 us
  waiting for transfers between devices  80.1 us (31%)
  Pallas kernels  52.7 us (20%)
  blocking collectives  51.2 us (20%)
  starting transfers between devices  41.6 us (16%)
  other arithmetic  14.3 us (6%)
  local copies, waits for them, and re-layouts  12.1 us (5%)
  matrix products  4.71 us (2%)
    all_to_all x1, blocking collectives, per_device(): late = jnp.sum(lax.all_to_all(late, 'freq', 0, 0, tiled=True), 0)  51.2 us
    all_to_all x1, waiting for transfers between devices, per_device(): lax.all_to_all(jnp.broadcast_to(energy[None], (16, classes, rows)), 'blk'...  24.2 us
    pallas_call x1, Pallas kernels, late_tiles(): pl.pallas_call(late_kernel, grid_spec=pltpu.PrefetchScalarGridSpec(num_sc...  23.7 us
    ppermute x15, starting transfers between devices, send(): return lax.ppermute(block, BOTH, route(dyh, dz, dc))  22.2 us
    all_to_all x1, waiting for transfers between devices, per_device(): lax.all_to_all(pieces, 'freq', 0, 0, tiled=True).reshape(2 * rows, rows)  15 us
    all_to_all x1, waiting for transfers between devices, per_device(): r1 = jnp.sum(lax.all_to_all(q1, 'freq', 0, 0, tiled=True), 0)  14.8 us
    ppermute x15, waiting for transfers between devices, send(): return lax.ppermute(block, BOTH, route(dyh, dz, dc))  14.1 us
    all_to_all x1, waiting for transfers between devices, per_device(): r4 = jnp.sum(lax.all_to_all(q4, 'freq', 0, 0, tiled=True), 0)  11.9 us
  transfers between devices with their start and end apart: 19, of which 9 were waited for; matrix products, arithmetic and copies ran while one was open for 7% of the time, Pallas kernels for 7%

profile of v2, /device:TPU:1, one launch (start us, length us, event | category | flops | bytes accessed | tf_op | source)
XLA Modules:
  0.0 256.9 jit_solution(14227424069118939484)
XLA Ops:
  3.4 6.7 %shard_map.55 = (bf16[320,4352]{1,0:T(8,128)(2,1)}, bf16[320,2176]{1,0:T(8,128)(2,1)}, bf16[320,2176]{1,0:T(8,128)(2,1)}, bf16[8,4352]{1,0:T(8,128)(2,1)}, f32[1,4352]{1,0:T(1,128)}) custom-call(s32[10]{0:T(128)} %stack.74.info, f32[28]{0:T(128)} %shell_weight.1, bf16[320,8]{1,0:T(8,128)(2,1)} %fusion.5.hot, bf16[320,4352]{1,0:T(8,128)(2,1)} %spectra.1, ...), custom_call_target="tpu_custom_call" | custom-call | tf_op jit(solution)/shard_map/pallas_call | solution.py:84
  11.5 3.0 %collective-permute-start = (bf16[320,2176]{1,0:T(8,128)(2,1)}, bf16[320,2176]{1,0:T(8,128)(2,1)}, u32[]{:S(2)}, u32[]{:S(2)}) collective-permute-start(bf16[320,2176]{1,0:T(8,128)(2,1)} %get-tuple-element.24), channel_id=1, source_target_pairs={{0,64},{1,65},{2,66},{3,67},{4,68},{5,69},{6,70},{7,71},{8,72},{9,... | collective-permute-start | bytes 4177928 | tf_op jit(solution)/shard_map/ppermute | solution.py:28
  16.9 4.7 %fusion = f32[8,320]{1,0:T(8,128)S(1)} fusion(bf16[8,4352]{1,0:T(8,128)(2,1)} %get-tuple-element.28, bf16[320,4352]{1,0:T(8,128)(2,1)} %get-tuple-element.26.a_mine.b.own.own_a, f32[4352]{0:T(1024)S(1)} %reduce), kind=kOutput, calls=%fused_computation | convolution fusion | flops 137871360 | bytes 2882560 | tf_op jit(solution)/shard_map/dot_general | solution.py:412
  23.2 9.3 %shard_map.56 = f32[8,80,320]{2,1,0:T(8,128)} custom-call(s32[10]{0:T(128)} %stack.74.info, bf16[320,4352]{1,0:T(8,128)(2,1)} %get-tuple-element.26.a_mine.b.own.own_a, bf16[320,4352]{1,0:T(8,128)(2,1)} %copy-done.1, bf16[320,4352]{1,0:T(8,128)(2,1)} %get-tuple-element.26.a_mine.b.own.own_a, f32[1,4352]{1,0:T(1,128)} %get-tuple-element.27.weight), custom_call_target="tpu_custom_call" | custom-call | tf_op jit(solution)/shard_map/pallas_call | solution.py:142
  32.6 2.4 pad_maximum_fusion
  35.0 4.3 %all-to-all-start = ((f32[8,88,320]{2,1,0:T(8,128)}), f32[8,88,320]{2,1,0:T(8,128)}, u32[]{:S(2)}, u32[]{:S(2)}) async-start(f32[8,88,320]{2,1,0:T(8,128)} %pad_maximum_fusion), calls=%async_computation | async-start | bytes 2162688 | tf_op jit(solution)/shard_map/all_to_all | solution.py:417
  39.3 2.2 collective-permute-start.3
  42.7 14.8 %all-to-all-done = f32[8,88,320]{2,1,0:T(8,128)} async-done(((f32[8,88,320]{2,1,0:T(8,128)}), f32[8,88,320]{2,1,0:T(8,128)}, u32[]{:S(2)}, u32[]{:S(2)}) %all-to-all-start) | async-done | bytes 901152 | tf_op jit(solution)/shard_map/all_to_all | solution.py:417
  64.2 6.6 %all-to-all-start.2 = ((f32[16,8,320]{2,1,0:T(8,128)}), f32[16,8,320]{2,1,0:T(8,128)S(1)}, u32[]{:S(2)}, u32[]{:S(2)}) async-start(f32[16,8,320]{2,1,0:T(8,128)} %broadcast_in_dim.264), calls=%async_computation.2 | async-start | bytes 393216 | tf_op jit(solution)/shard_map/all_to_all | solution.py:428
  71.6 8.0 %shard_map.57 = f32[8,80,320]{2,1,0:T(8,128)} custom-call(s32[10]{0:T(128)} %stack.74.info, bf16[320,4352]{1,0:T(8,128)(2,1)} %get-tuple-element.26.a_mine.b.own.own_a, bf16[320,4352]{1,0:T(8,128)(2,1)} %get-tuple-element.26.a_mine.b.own.own_a, bf16[320,4352]{1,0:T(8,128)(2,1)} %copy-done.1, ...), custom_call_target="tpu_custom_call" | custom-call | tf_op jit(solution)/shard_map/pallas_call | solution.py:185
  79.6 24.2 %all-to-all-done.2 = f32[16,8,320]{2,1,0:T(8,128)S(1)} async-done(((f32[16,8,320]{2,1,0:T(8,128)}), f32[16,8,320]{2,1,0:T(8,128)S(1)}, u32[]{:S(2)}, u32[]{:S(2)}) %all-to-all-start.2) | async-done | bytes 163872 | tf_op jit(solution)/shard_map/all_to_all | solution.py:428
  103.8 5.0 %all-to-all-start.1 = ((f32[8,80,320]{2,1,0:T(8,128)}), f32[8,80,320]{2,1,0:T(8,128)}, u32[]{:S(2)}, u32[]{:S(2)}) async-start(f32[8,80,320]{2,1,0:T(8,128)} %shard_map.57), calls=%async_computation.1 | async-start | bytes 1966080 | tf_op jit(solution)/shard_map/all_to_all | solution.py:427
  109.0 3.1 %add_sqrt_fusion.root = f32[320,640]{1,0:T(8,128)} fusion(f32[640]{0:T(1024)S(1)} %get-tuple-element.49, f32[640]{0:T(1024)S(1)} %get-tuple-element.50, f32[640]{0:T(1024)S(1)} %get-tuple-element.48, f32[640]{0:T(1024)S(1)} %get-tuple-element.47, f32[640]{0:T(1024)S(1)} %get-tuple-element.46, f32[640]{0:T(1024)S(1)} %get-tuple-element.45, ...), kind=kLoop, calls=%fused_computation.6 | loop fusion | flops 3686400 | bytes 857600 | tf_op jit(solution)/shard_map/sqrt | solution.py:437
  112.1 11.9 %all-to-all-done.1 = f32[8,80,320]{2,1,0:T(8,128)} async-done(((f32[8,80,320]{2,1,0:T(8,128)}), f32[8,80,320]{2,1,0:T(8,128)}, u32[]{:S(2)}, u32[]{:S(2)}) %all-to-all-start.1) | async-done | bytes 819232 | tf_op jit(solution)/shard_map/all_to_all | solution.py:427
  126.7 6.5 %collective-permute-done.8.previous_other = bf16[320,2176]{1,0:T(8,128)(2,1)S(1)} collective-permute-done((bf16[320,2176]{1,0:T(8,128)(2,1)}, bf16[320,2176]{1,0:T(8,128)(2,1)S(1)}, u32[]{:S(2)}, u32[]{:S(2)}) %collective-permute-start.8) | collective-permute-done | bytes 1392672 | tf_op jit(solution)/shard_map/ppermute | solution.py:28
  137.8 23.7 %shard_map.58 = f32[8,4,80,320]{3,2,1,0:T(8,128)} custom-call(s32[10]{0:T(128)} %stack.74.info, bf16[320,4352]{1,0:T(8,128)(2,1)} %get-tuple-element.26.a_mine.b.own.own_a, bf16[320,2176]{1,0:T(8,128)(2,1)} %collective-permute-done.partner.partner_a.near_half, bf16[320,2176]{1,0:T(8,128)(2,1)} %collective-permute-done.5.far_half, ...), custom_call_target="tpu_custom_call" | custom-call | tf_op jit(solution)/shard_map/pallas_call | solution.py:280
  161.5 51.2 %all_to_all.25 = f32[8,4,80,320]{3,2,1,0:T(8,128)} all-to-all(f32[8,4,80,320]{3,2,1,0:T(8,128)} %shard_map.58), channel_id=1, replica_groups=mesh['blk'=16,'freq'=8] {'freq'}, dimensions={0} | all-to-all | bytes 6553600 | tf_op jit(solution)/shard_map/all_to_all | solution.py:445
  212.7 2.4 reduce_sum.29
  215.1 2.4 collective-permute-start.10
  223.3 5.3 %collective-permute-done.13.from_diagonal = f32[80,320]{1,0:T(8,128)S(1)} collective-permute-done((f32[80,320]{1,0:T(8,128)S(1)}, f32[80,320]{1,0:T(8,128)S(1)}, u32[]{:S(2)}, u32[]{:S(2)}) %collective-permute-start.13) | collective-permute-done | bytes 102432 | tf_op jit(solution)/shard_map/ppermute | solution.py:28
  230.0 2.3 shard_map.59
  232.3 3.6 %all-to-all-start.4 = ((f32[8,80,320]{2,1,0:T(8,128)}), f32[8,80,320]{2,1,0:T(8,128)S(1)}, u32[]{:S(2)}, u32[]{:S(2)}) async-start(f32[8,80,320]{2,1,0:T(8,128)} %shard_map.59), calls=%async_computation.4 | async-start | bytes 1966080 | tf_op jit(solution)/shard_map/all_to_all | solution.py:455
  235.9 15.0 %all-to-all-done.4 = f32[8,80,320]{2,1,0:T(8,128)S(1)} async-done(((f32[8,80,320]{2,1,0:T(8,128)}), f32[8,80,320]{2,1,0:T(8,128)S(1)}, u32[]{:S(2)}, u32[]{:S(2)}) %all-to-all-start.4) | async-done | bytes 819232 | tf_op jit(solution)/shard_map/all_to_all | solution.py:455
  254.2 2.7 %shard_map.60 = f32[320,640]{1,0:T(8,128)} custom-call(s32[2]{0:T(128)} %pad_add_fusion.info, f32[640,320]{1,0:T(8,128)} %bitcast.25, f32[320,320]{1,0:T(8,128)} %copy-done.7, f32[320,640]{1,0:T(8,128)} %add_sqrt_fusion.root), custom_call_target="tpu_custom_call" | custom-call | tf_op jit(solution)/shard_map/pallas_call | solution.py:363
  (70 shorter events, 35.4 us)
Async XLA Ops:
  10.1 11.5 %collective-permute-start.2 = (bf16[320,4352]{1,0:T(8,128)(2,1)}, bf16[320,4352]{1,0:T(8,128)(2,1)S(1)}, u32[]{:S(2)}, u32[]{:S(2)}) collective-permute-start(bf16[320,4352]{1,0:T(8,128)(2,1)} %get-tuple-element.26.a_mine.b.own.own_a), channel_id=1, source_target_pairs={{0,8},{1,9},{2,10},{3,11},{4,12},{5,13},{6,14},{7,15},{8,0},{9,1},... | collective-permute-start | bytes 8355848 | tf_op jit(solution)/shard_map/ppermute | solution.py:28
  11.5 47.9 %collective-permute-start = (bf16[320,2176]{1,0:T(8,128)(2,1)}, bf16[320,2176]{1,0:T(8,128)(2,1)}, u32[]{:S(2)}, u32[]{:S(2)}) collective-permute-start(bf16[320,2176]{1,0:T(8,128)(2,1)} %get-tuple-element.24), channel_id=1, source_target_pairs={{0,64},{1,65},{2,66},{3,67},{4,68},{5,69},{6,70},{7,71},{8,72},{9,... | collective-permute-start | bytes 4177928 | tf_op jit(solution)/shard_map/ppermute | solution.py:28
  14.5 44.9 %collective-permute-start.1 = (bf16[320,2176]{1,0:T(8,128)(2,1)}, bf16[320,2176]{1,0:T(8,128)(2,1)}, u32[]{:S(2)}, u32[]{:S(2)}) collective-permute-start(bf16[320,2176]{1,0:T(8,128)(2,1)} %get-tuple-element.25), channel_id=1, source_target_pairs={{0,16},{1,17},{2,18},{3,19},{4,20},{5,21},{6,22},{7,23},{8,24},{9,... | collective-permute-start | bytes 4177928 | tf_op jit(solution)/shard_map/ppermute | solution.py:28
  21.7 1.6 copy-start.1
  32.6 6.7 %copy-start = (bf16[320,4352]{1,0:T(8,128)(2,1)S(1)}, bf16[320,4352]{1,0:T(8,128)(2,1)}, u32[]{:S(2)}) copy-start(bf16[320,4352]{1,0:T(8,128)(2,1)} %get-tuple-element.26.a_mine.b.own.own_a) | copy-start | bytes 8355844
  35.0 22.4 %all-to-all-start = ((f32[8,88,320]{2,1,0:T(8,128)}), f32[8,88,320]{2,1,0:T(8,128)}, u32[]{:S(2)}, u32[]{:S(2)}) async-start(f32[8,88,320]{2,1,0:T(8,128)} %pad_maximum_fusion), calls=%async_computation | async-start | bytes 2162688 | tf_op jit(solution)/shard_map/all_to_all | solution.py:417
  39.3 86.0 %collective-permute-start.3 = (bf16[320,4352]{1,0:T(8,128)(2,1)S(1)}, bf16[320,4352]{1,0:T(8,128)(2,1)}, u32[]{:S(2)}, u32[]{:S(2)}) collective-permute-start(bf16[320,4352]{1,0:T(8,128)(2,1)S(1)} %copy-done), channel_id=1, source_target_pairs={{0,48},{1,49},{2,50},{3,51},{4,52},{5,53},{6,54},{7,55},{8,56},{9,... | collective-permute-start | bytes 8355848 | tf_op jit(solution)/shard_map/ppermute | solution.py:28
  59.5 12.2 %collective-permute-start.6 = (bf16[320,2176]{1,0:T(8,128)(2,1)}, bf16[320,2176]{1,0:T(8,128)(2,1)}, u32[]{:S(2)}, u32[]{:S(2)}) collective-permute-start(bf16[320,2176]{1,0:T(8,128)(2,1)} %collective-permute-done.partner.partner_a.near_half), channel_id=1, source_target_pairs={{0,8},{1,9},{2,10},{3,11},{4,12},{5,13},{6,14},{7,15},{8,0},{9,1},... | collective-permute-start | bytes 4177928 | tf_op jit(solution)/shard_map/ppermute | solution.py:28
  60.3 65.0 %collective-permute-start.5 = (bf16[320,2176]{1,0:T(8,128)(2,1)}, bf16[320,2176]{1,0:T(8,128)(2,1)}, u32[]{:S(2)}, u32[]{:S(2)}) collective-permute-start(bf16[320,2176]{1,0:T(8,128)(2,1)} %constant_dynamic-slice_fusion.1), channel_id=1, source_target_pairs={{0,64},{1,65},{2,66},{3,67},{4,68},{5,69},{6,70},{7,71},{8,72},{9,... | collective-permute-start | bytes 4177928 | tf_op jit(solution)/shard_map/ppermute | solution.py:28
  61.9 63.4 %collective-permute-start.4 = (bf16[320,2176]{1,0:T(8,128)(2,1)}, bf16[320,2176]{1,0:T(8,128)(2,1)}, u32[]{:S(2)}, u32[]{:S(2)}) collective-permute-start(bf16[320,2176]{1,0:T(8,128)(2,1)} %collective-permute-done.partner.partner_a.near_half), channel_id=1, source_target_pairs={{0,16},{1,17},{2,18},{3,19},{4,20},{5,21},{6,22},{7,23},{8,24},{9,... | collective-permute-start | bytes 4177928 | tf_op jit(solution)/shard_map/ppermute | solution.py:28
  64.2 39.6 %all-to-all-start.2 = ((f32[16,8,320]{2,1,0:T(8,128)}), f32[16,8,320]{2,1,0:T(8,128)S(1)}, u32[]{:S(2)}, u32[]{:S(2)}) async-start(f32[16,8,320]{2,1,0:T(8,128)} %broadcast_in_dim.264), calls=%async_computation.2 | async-start | bytes 393216 | tf_op jit(solution)/shard_map/all_to_all | solution.py:428
  103.8 20.2 %all-to-all-start.1 = ((f32[8,80,320]{2,1,0:T(8,128)}), f32[8,80,320]{2,1,0:T(8,128)}, u32[]{:S(2)}, u32[]{:S(2)}) async-start(f32[8,80,320]{2,1,0:T(8,128)} %shard_map.57), calls=%async_computation.1 | async-start | bytes 1966080 | tf_op jit(solution)/shard_map/all_to_all | solution.py:427
  125.3 93.0 %copy-start.6 = (f32[80,320]{1,0:T(8,128)}, f32[80,320]{1,0:T(8,128)S(1)}, u32[]{:S(2)}) copy-start(f32[80,320]{1,0:T(8,128)S(1)} %reduce_sum.28.r4) | copy-start | bytes 307204
  125.3 11.0 %collective-permute-start.7 = (bf16[320,4352]{1,0:T(8,128)(2,1)}, bf16[320,4352]{1,0:T(8,128)(2,1)S(1)}, u32[]{:S(2)}, u32[]{:S(2)}) collective-permute-start(bf16[320,4352]{1,0:T(8,128)(2,1)} %collective-permute-done.3.following_high.following_yh.a_mine), channel_id=1, source_target_pairs={{0,8},{1,9},{2,10},{3,11},{4,12},{5,13},{6,14},{7,15},{8,0},{9,1},... | collective-permute-start | bytes 8355848 | tf_op jit(solution)/shard_map/ppermute | solution.py:28
  126.2 7.0 %collective-permute-start.8 = (bf16[320,2176]{1,0:T(8,128)(2,1)}, bf16[320,2176]{1,0:T(8,128)(2,1)S(1)}, u32[]{:S(2)}, u32[]{:S(2)}) collective-permute-start(bf16[320,2176]{1,0:T(8,128)(2,1)} %collective-permute-done.1.previous.previous_mine), channel_id=1, source_target_pairs={{0,8},{1,9},{2,10},{3,11},{4,12},{5,13},{6,14},{7,15},{8,0},{9,1},... | collective-permute-start | bytes 4177928 | tf_op jit(solution)/shard_map/ppermute | solution.py:28
  126.3 8.9 %collective-permute-start.9 = (bf16[320,2176]{1,0:T(8,128)(2,1)}, bf16[320,2176]{1,0:T(8,128)(2,1)S(1)}, u32[]{:S(2)}, u32[]{:S(2)}) collective-permute-start(bf16[320,2176]{1,0:T(8,128)(2,1)} %collective-permute-done.4.diagonal.diagonal_mine), channel_id=1, source_target_pairs={{0,8},{1,9},{2,10},{3,11},{4,12},{5,13},{6,14},{7,15},{8,0},{9,1},... | collective-permute-start | bytes 4177928 | tf_op jit(solution)/shard_map/ppermute | solution.py:28
  136.3 1.5 copy-start.3
  215.1 14.1 %collective-permute-start.10 = (f32[4,80,320]{2,1,0:T(8,128)S(1)}, f32[4,80,320]{2,1,0:T(8,128)S(1)}, u32[]{:S(2)}, u32[]{:S(2)}) collective-permute-start(f32[4,80,320]{2,1,0:T(8,128)S(1)} %reduce_sum.29), channel_id=1, source_target_pairs={{0,16},{1,17},{2,18},{3,19},{4,20},{5,21},{6,22},{7,23},{8,24},{9,... | collective-permute-start | bytes 1228808 | tf_op jit(solution)/shard_map/ppermute | solution.py:28
  218.3 10.3 %collective-permute-start.12 = (f32[2,80,320]{2,1,0:T(8,128)S(1)}, f32[2,80,320]{2,1,0:T(8,128)S(1)}, u32[]{:S(2)}, u32[]{:S(2)}) collective-permute-start(f32[2,80,320]{2,1,0:T(8,128)S(1)} %pad_maximum_fusion.1), channel_id=1, source_target_pairs={{0,64},{1,65},{2,66},{3,67},{4,68},{5,69},{6,70},{7,71},{8,72},{9,... | collective-permute-start | bytes 614408 | tf_op jit(solution)/shard_map/ppermute | solution.py:28
  219.8 8.8 %collective-permute-start.13 = (f32[80,320]{1,0:T(8,128)S(1)}, f32[80,320]{1,0:T(8,128)S(1)}, u32[]{:S(2)}, u32[]{:S(2)}) collective-permute-start(f32[80,320]{1,0:T(8,128)S(1)} %get-tuple-element.61), channel_id=1, source_target_pairs={{0,112},{1,113},{2,114},{3,115},{4,116},{5,117},{6,118},{7,119},{8... | collective-permute-start | bytes 307208 | tf_op jit(solution)/shard_map/ppermute | solution.py:28
  221.9 6.7 %collective-permute-start.11 = (f32[80,320]{1,0:T(8,128)S(1)}, f32[80,320]{1,0:T(8,128)S(1)}, u32[]{:S(2)}, u32[]{:S(2)}) collective-permute-start(f32[80,320]{1,0:T(8,128)S(1)} %get-tuple-element.63), channel_id=1, source_target_pairs={{0,48},{1,49},{2,50},{3,51},{4,52},{5,53},{6,54},{7,55},{8,56},{9,... | collective-permute-start | bytes 307208 | tf_op jit(solution)/shard_map/ppermute | solution.py:28
  232.3 18.6 %all-to-all-start.4 = ((f32[8,80,320]{2,1,0:T(8,128)}), f32[8,80,320]{2,1,0:T(8,128)S(1)}, u32[]{:S(2)}, u32[]{:S(2)}) async-start(f32[8,80,320]{2,1,0:T(8,128)} %shard_map.59), calls=%async_computation.4 | async-start | bytes 1966080 | tf_op jit(solution)/shard_map/all_to_all | solution.py:455
  250.9 2.5 copy-start.2
  250.9 2.4 collective-permute-start.14
  (7 other events, 5.9 us)
